TPU v7x, 512 devices: a whole 4x8x8 slice. The times are simulated.
512 devices in a mesh: ctx: 128 (over z, y, core), rep: 4 (over x).
Axes of the slice: x: 4, y: 8, z: 8, core: 2. Of those that a mesh axis runs over, the one named last changes fastest.
Arguments:
- offsets: int32 [4, 17], P('rep'), may hold values from 0 to 32768, as said below
- pairs: int32 [4, 1280, 2], P('rep', 'ctx'), may hold values from 0 to 5, as said below
- pair_count: int32 [4, 128], P('rep', 'ctx'), may hold values from 2 to 10, as said below
- queries: bfloat16 [4, 32768, 1024], P('rep', 'ctx'), may hold values from -6 to 6
- keys: bfloat16 [4, 32768, 1024], P('rep', 'ctx'), may hold values from -6 to 6
- values: bfloat16 [4, 32768, 1024], P('rep', 'ctx'), may hold values from -6 to 6
- cotangent: bfloat16 [4, 32768, 1024], P('rep', 'ctx'), may hold values from -6 to 6
- alpha: float32 [8], replicated, may hold values from 0.5 to 2
Outputs:
- attended: bfloat16 [4, 32768, 1024], P('rep', 'ctx')
- grad_queries: bfloat16 [4, 32768, 1024], P('rep', 'ctx')
- grad_keys: bfloat16 [4, 32768, 1024], P('rep', 'ctx')
- grad_values: bfloat16 [4, 32768, 1024], P('rep', 'ctx')
- grad_alpha: float32 [8], replicated
Inputs may be any that keep to these rules, and one draw needn't show every extreme that they name: Per batch: offsets start at 0, never fall and end at 32768; every user holds at most 16384 events, one holds exactly 16384; some users may be empty. `pairs`: rows c * 10 to (c + 1) * 10 - 1 belong to ctx device c. For each of the device's query blocks a (0 to 1, in order) they list (a, b) for every key block from the block holding the later of two rows, the first event of the user of the query block's first row and that first row plus 1 minus 512, up to the query block itself; b counts blocks from the first block of device c - 2. Entries past pair_count are zero. Every pair holding a row pair with mask 1 is listed. `pair_count`: the number of listed pairs of each device, at least one for each query block; some device lists 10.
All inputs are finite; a program needn't handle non-finite values.
Results may differ from a plain program's by a relative error of at most 0.0049.
Values may be sent and summed in bfloat16 or wider, within the bound.
A program may use at most 64 MiB of HBM per device.

v0:
```python
import math

import jax
import jax.numpy as jnp
from jax import lax
from jax.sharding import PartitionSpec as P

BLOCK = 128
WINDOW = 512


def from_behind(block, axis, distance):
    devices = range(lax.axis_size(axis))
    route = [(i - distance, i) for i in devices if i - distance in devices]
    return lax.ppermute(block, axis, route)


def user_index(offsets_one, row_ids):
    return jnp.sum((offsets_one[None, :] <= row_ids[:, None]).astype(jnp.int32), axis=1) - 1


def row_scale(offsets_one, users):
    lengths = offsets_one[1:] - offsets_one[:-1]
    labels = jnp.arange(lengths.shape[0], dtype=jnp.int32)
    counted = jnp.sum(jnp.where(users[:, None] == labels[None, :], lengths[None, :], 0), axis=1)
    return lax.rsqrt(jnp.minimum(counted, WINDOW).astype(jnp.float32))


def add_block(total, first, term):
    current = lax.dynamic_slice_in_dim(total, first, term.shape[0], 0)
    return lax.dynamic_update_slice_in_dim(total, current + term, first, 0)


def tile_terms(query_blk, key_blk, value_blk, grad_blk, weight, alpha):
    heads = alpha.shape[0]
    block = query_blk.shape[0]
    coeff = 1.0 / math.sqrt(query_blk.shape[1] // heads)
    shaped_q = query_blk.reshape(block, heads, -1)
    shaped_k = key_blk.reshape(block, heads, -1)
    shaped_v = value_blk.reshape(block, heads, -1)
    shaped_g = grad_blk.reshape(block, heads, -1)
    raw = jnp.einsum("qhd,khd->hqk", shaped_q, shaped_k, preferred_element_type=jnp.float32) * coeff
    scores = alpha[:, None, None] * raw
    sigma = jax.nn.sigmoid(scores)
    attend = (scores * sigma * weight[None]).astype(jnp.bfloat16)
    grad_attend = jnp.einsum("qhd,khd->hqk", shaped_g, shaped_v, preferred_element_type=jnp.float32)
    grad_scores = grad_attend * weight[None] * sigma * (1.0 + scores * (1.0 - sigma))
    grad_raw = (grad_scores * (alpha[:, None, None] * coeff)).astype(jnp.bfloat16)
    grad_value = jnp.einsum(
        "hqk,qhd->khd", attend, shaped_g, preferred_element_type=jnp.float32
    ).reshape(block, -1)
    grad_key = jnp.einsum(
        "hqk,qhd->khd", grad_raw, shaped_q, preferred_element_type=jnp.float32
    ).reshape(block, -1)
    output = jnp.einsum(
        "hqk,khd->qhd", attend, shaped_v, preferred_element_type=jnp.float32
    ).reshape(block, -1)
    grad_query = jnp.einsum(
        "hqk,khd->qhd", grad_raw, shaped_k, preferred_element_type=jnp.float32
    ).reshape(block, -1)
    grad_alpha = jnp.sum(grad_scores * raw, axis=(1, 2))
    return (output, grad_query, grad_key, grad_value, grad_alpha)


def run_pairs(
    plist,
    count,
    queries_own,
    grads_own,
    keys_win,
    values_win,
    q_users,
    q_rows,
    q_scale,
    k_users,
    k_rows,
    alpha,
):
    rows, width = queries_own.shape
    span = keys_win.shape[0]

    def one_pair(index, carry):
        query_first = plist[index, 0] * BLOCK
        key_first = plist[index, 1] * BLOCK

        def take_query(array):
            return lax.dynamic_slice_in_dim(array, query_first, BLOCK, 0)

        def take_key(array):
            return lax.dynamic_slice_in_dim(array, key_first, BLOCK, 0)

        apart = take_query(q_rows)[:, None] - take_key(k_rows)[None, :]
        mask = (
            (take_query(q_users)[:, None] == take_key(k_users)[None, :])
            & (apart >= 0)
            & (apart < WINDOW)
        )
        weight = jnp.where(mask, take_query(q_scale)[:, None], jnp.zeros((), jnp.float32))
        out_acc, dq_acc, dk_acc, dv_acc, da_acc = carry
        terms = tile_terms(
            take_query(queries_own),
            take_key(keys_win),
            take_key(values_win),
            take_query(grads_own),
            weight,
            alpha,
        )
        out_acc = add_block(out_acc, query_first, terms[0])
        dq_acc = add_block(dq_acc, query_first, terms[1])
        dk_acc = add_block(dk_acc, key_first, terms[2])
        dv_acc = add_block(dv_acc, key_first, terms[3])
        return (out_acc, dq_acc, dk_acc, dv_acc, da_acc + terms[4])

    init = (
        jnp.zeros((rows, width), jnp.float32),
        jnp.zeros((rows, width), jnp.float32),
        jnp.zeros((span, width), jnp.float32),
        jnp.zeros((span, width), jnp.float32),
        jnp.zeros(alpha.shape, jnp.float32),
    )
    return lax.fori_loop(0, count, one_pair, init)


def shards(offsets, pairs, pair_count, queries, keys, values, cotangent, alpha):
    offsets_one = offsets[0]
    plist = pairs[0]
    count = pair_count[0, 0]
    queries_own = queries[0]
    grads_own = cotangent[0]
    rows, width = queries_own.shape
    depth = (WINDOW - 2) // rows + 1
    device = lax.axis_index("ctx")
    packed = jnp.stack([keys[0], values[0]])
    pieces = []
    for distance in range(depth, 0, -1):
        pieces.append(from_behind(packed, "ctx", distance))
    window = jnp.concatenate(pieces + [packed], axis=1)
    q_rows = device * rows + jnp.arange(rows, dtype=jnp.int32)
    k_rows = (device - depth) * rows + jnp.arange((depth + 1) * rows, dtype=jnp.int32)
    q_users = user_index(offsets_one, q_rows)
    k_users = user_index(offsets_one, k_rows)
    q_scale = row_scale(offsets_one, q_users)
    out_acc, dq_acc, dk_acc, dv_acc, da_acc = run_pairs(
        plist,
        count,
        queries_own,
        grads_own,
        window[0],
        window[1],
        q_users,
        q_rows,
        q_scale,
        k_users,
        k_rows,
        alpha,
    )
    partial_kv = jnp.stack([dk_acc, dv_acc])
    owned = partial_kv[:, depth * rows :]
    for distance in range(1, depth + 1):
        segment = partial_kv[:, (depth - distance) * rows : (depth - distance + 1) * rows]
        owned = owned + from_behind(segment, "ctx", -distance)
    key_grad_own, value_grad_own = (owned[0], owned[1])
    grad_alpha = lax.psum(da_acc, ("ctx", "rep"))
    return (
        out_acc.astype(jnp.bfloat16)[None],
        dq_acc.astype(jnp.bfloat16)[None],
        key_grad_own.astype(jnp.bfloat16)[None],
        value_grad_own.astype(jnp.bfloat16)[None],
        grad_alpha,
    )


def solution(mesh):
    return jax.shard_map(
        shards,
        mesh=mesh,
        in_specs=(
            P("rep", None),
            P("rep", "ctx", None),
            P("rep", "ctx"),
            P("rep", "ctx", None),
            P("rep", "ctx", None),
            P("rep", "ctx", None),
            P("rep", "ctx", None),
            P(),
        ),
        out_specs=(
            P("rep", "ctx", None),
            P("rep", "ctx", None),
            P("rep", "ctx", None),
            P("rep", "ctx", None),
            P(),
        ),
        check_vma=False,
    )
```

profile of v0, /device:TPU:1, one launch (start us, length us, event | category | flops | bytes accessed | tf_op | source)
XLA Modules:
  0.0 400.6 jit_solution(3446915070380144915)
XLA Ops:
  2.8 4.6 %collective-permute-start.1 = (bf16[2,256,1024]{2,1,0:T(8,128)(2,1)S(1)}, bf16[2,256,1024]{2,1,0:T(8,128)(2,1)S(1)}, u32[]{:S(2)}, u32[]{:S(2)}) collective-permute-start(bf16[2,256,1024]{2,1,0:T(8,128)(2,1)S(1)} %constant_dynamic-update-slice_fusion.4), channel_id=1, source_target_pairs={{0,4},{4,8},{8,12},{12,16},{16,20},{20,24},{24,28},{28,32},{32,36}... | collective-permute-start | bytes 3145736 | tf_op jit(solution)/shard_map/ppermute | solution.py:15
  7.4 3.3 collective-permute-start
  11.5 2.0 copy.37
  13.5 2.0 copy.38
  15.9 9.3 %collective-permute-done.1 = bf16[2,256,1024]{2,1,0:T(8,128)(2,1)S(1)} collective-permute-done((bf16[2,256,1024]{2,1,0:T(8,128)(2,1)S(1)}, bf16[2,256,1024]{2,1,0:T(8,128)(2,1)S(1)}, u32[]{:S(2)}, u32[]{:S(2)}) %collective-permute-start.1) | collective-permute-done | bytes 1048608 | tf_op jit(solution)/shard_map/ppermute | solution.py:15
  25.2 16.4 %collective-permute-done = bf16[2,256,1024]{2,1,0:T(8,128)(2,1)S(1)} collective-permute-done((bf16[2,256,1024]{2,1,0:T(8,128)(2,1)S(1)}, bf16[2,256,1024]{2,1,0:T(8,128)(2,1)S(1)}, u32[]{:S(2)}, u32[]{:S(2)}) %collective-permute-start) | collective-permute-done | bytes 1048608 | tf_op jit(solution)/shard_map/ppermute | solution.py:15
  41.9 2.0 slice_bitcast_fusion
  43.9 1.1 broadcast.104.clone2
  45.0 1.1 broadcast.104.clone
  46.1 2.1 broadcast.105.clone2
  48.2 2.0 broadcast.105.clone
  50.2 117.7 %while.18 = (s32[]{:T(128)}, f32[256,1024]{1,0:T(8,128)}, f32[256,1024]{1,0:T(8,128)}, f32[768,1024]{1,0:T(8,128)}, f32[768,1024]{1,0:T(8,128)}, /*index=5*/f32[...) while((s32[]{:T(128)}, f32[256,1024]{1,0:T(8,128)}, ...), condition=%wide.region_5.6_spmd, body=%wide.region_3.5_spmd.sunk | while | flops 204587040 | bytes 38150372 | solution.py:121
  60.1 1.1 constant_dynamic-slice_fusion.20
  76.9 1.1 constant_dynamic-slice_fusion.20
  78.4 1.1 constant_dynamic-slice_fusion.27
  128.6 1.1 constant_dynamic-slice_fusion.27
  130.2 1.1 constant_dynamic-slice_fusion.26
  146.9 1.1 constant_dynamic-slice_fusion.26
  167.9 4.8 %fusion.7 = (f32[2,256,1024]{2,1,0:T(8,128)}, f32[2,256,1024]{2,1,0:T(8,128)}) fusion(f32[1,768,1024]{2,1,0:T(8,128)} %bitcast.95, f32[1,768,1024]{2,1,0:T(8,128)} %bitcast.93), kind=kLoop, calls=%fused_computation.38 | loop fusion | flops 1048576 | bytes 10485760 | tf_op jit(solution)/shard_map/stack | solution.py:157
  172.7 2.2 collective-permute-start.2
  174.9 1.3 collective-permute-start.3
  176.2 217.7 %psum.7 = f32[8]{0:T(128)} all-reduce(f32[8]{0:T(128)S(1)} %get-tuple-element.106), channel_id=1, replica_groups=mesh['ctx'=128,'rep'=4] {'ctx','rep'}, use_global_device_ids=true, to_apply=%region_6.7 | all-reduce | flops 8 | bytes 64 | tf_op jit(solution)/shard_map/psum | solution.py:163
  393.9 2.7 convert_bitcast_fusion
  396.6 3.0 fusion.11
  (305 shorter events, 100.0 us)
Async XLA Ops:
  0.6 15.0 %copy-start.3 = (s32[1,17]{1,0:T(1,128)S(1)}, s32[1,17]{1,0:T(1,128)}, u32[]{:S(2)}) copy-start(s32[1,17]{1,0:T(1,128)} %param.10) | copy-start | bytes 208
  2.8 22.4 %collective-permute-start.1 = (bf16[2,256,1024]{2,1,0:T(8,128)(2,1)S(1)}, bf16[2,256,1024]{2,1,0:T(8,128)(2,1)S(1)}, u32[]{:S(2)}, u32[]{:S(2)}) collective-permute-start(bf16[2,256,1024]{2,1,0:T(8,128)(2,1)S(1)} %constant_dynamic-update-slice_fusion.4), channel_id=1, source_target_pairs={{0,4},{4,8},{8,12},{12,16},{16,20},{20,24},{24,28},{28,32},{32,36}... | collective-permute-start | bytes 3145736 | tf_op jit(solution)/shard_map/ppermute | solution.py:15
  7.4 34.2 %collective-permute-start = (bf16[2,256,1024]{2,1,0:T(8,128)(2,1)S(1)}, bf16[2,256,1024]{2,1,0:T(8,128)(2,1)S(1)}, u32[]{:S(2)}, u32[]{:S(2)}) collective-permute-start(bf16[2,256,1024]{2,1,0:T(8,128)(2,1)S(1)} %constant_dynamic-update-slice_fusion.4), channel_id=1, source_target_pairs={{0,8},{4,12},{8,16},{12,20},{16,24},{20,28},{24,32},{28,36},{32,40... | collective-permute-start | bytes 3145736 | tf_op jit(solution)/shard_map/ppermute | solution.py:15
  46.1 4.1 %copy-start.2 = (s32[1,10,2]{1,2,0:T(2,128)S(1)}, s32[1,10,2]{1,2,0:T(2,128)}, u32[]{:S(2)}) copy-start(s32[1,10,2]{1,2,0:T(2,128)} %param.11) | copy-start | bytes 244
  46.1 4.1 %copy-start.4 = (f32[8]{0:T(128)S(1)}, f32[8]{0:T(128)}, u32[]{:S(2)}) copy-start(f32[8]{0:T(128)} %param.17) | copy-start | bytes 100
  58.4 1.2 copy-start.1
  75.1 1.2 copy-start.1
  91.9 1.2 copy-start.1
  108.6 1.2 copy-start.1
  125.3 1.2 copy-start.1
  142.0 1.2 copy-start.1
  158.7 1.2 copy-start.1
  172.7 223.8 %copy-start = (f32[768,1024]{1,0:T(8,128)S(1)}, f32[768,1024]{1,0:T(8,128)}, u32[]{:S(2)}) copy-start(f32[768,1024]{1,0:T(8,128)} %get-tuple-element.105) | copy-start | bytes 9437188
  172.7 223.8 %collective-permute-start.2 = (f32[2,256,1024]{2,1,0:T(8,128)}, f32[2,256,1024]{2,1,0:T(8,128)}, u32[]{:S(2)}, u32[]{:S(2)}) collective-permute-start(f32[2,256,1024]{2,1,0:T(8,128)} %get-tuple-element.188), channel_id=1, source_target_pairs={{4,0},{8,4},{12,8},{16,12},{20,16},{24,20},{28,24},{32,28},{36,32}... | collective-permute-start | bytes 6291464 | tf_op jit(solution)/shard_map/ppermute | solution.py:15
  174.9 221.6 %collective-permute-start.3 = (f32[2,256,1024]{2,1,0:T(8,128)}, f32[2,256,1024]{2,1,0:T(8,128)}, u32[]{:S(2)}, u32[]{:S(2)}) collective-permute-start(f32[2,256,1024]{2,1,0:T(8,128)} %get-tuple-element.189), channel_id=1, source_target_pairs={{8,0},{12,4},{16,8},{20,12},{24,16},{28,20},{32,24},{36,28},{40,32... | collective-permute-start | bytes 6291464 | tf_op jit(solution)/shard_map/ppermute | solution.py:15
where the time goes:
time: 404 us; the launch traced here: 401 us
  blocking collectives  218 us (54%)
  local copies, waits for them, and re-layouts  101 us (25%)
  waiting for transfers between devices  25.7 us (6%)
  loops' own time  15.8 us (4%)
  other arithmetic  14.3 us (4%)
  matrix products  14.3 us (4%)
  starting transfers between devices  11.3 us (3%)
    psum x1, blocking collectives, shards(): grad_alpha = lax.psum(da_acc, ('ctx', 'rep'))  218 us
    dynamic_slice x56, local copies, waits for them, and re-layouts, add_block(): current = lax.dynamic_slice_in_dim(total, first, term.shape[0], 0)  28.4 us
    ppermute x4, waiting for transfers between devices, from_behind(): return lax.ppermute(block, axis, route)  25.7 us
    dynamic_update_slice x42, local copies, waits for them, and re-layouts, add_block(): return lax.dynamic_update_slice_in_dim(total, current + term, first, 0)  20.3 us
    dynamic_slice x42, local copies, waits for them, and re-layouts, take_key(): return lax.dynamic_slice_in_dim(array, key_first, BLOCK, 0)  17 us
    another operation x1, loops' own time, run_pairs(): return lax.fori_loop(0, count, one_pair, init)  15.8 us
    dynamic_slice x35, local copies, waits for them, and re-layouts, take_query(): return lax.dynamic_slice_in_dim(array, query_first, BLOCK, 0)  15.2 us
    ppermute x4, starting transfers between devices, from_behind(): return lax.ppermute(block, axis, route)  11.3 us
  transfers between devices with their start and end apart: 4, of which 2 were waited for; matrix products, arithmetic and copies ran while one was open for 2% of the time, Pallas kernels for 0%

commit v1 on v0

v1 whole, which is shorter than its diff:
```python
import math

import jax
import jax.numpy as jnp
from jax import lax
from jax.experimental import pallas as pl
from jax.experimental.pallas import tpu as pltpu
from jax.sharding import PartitionSpec as P

WINDOW = 512
HEAD = 128
STRIP = 32
AHEAD = 4
LINE = 8
MESH = pl.DeviceIdType.MESH


def row_facts(offsets_ref, users, rows):
    start = jnp.zeros_like(rows)
    end = jnp.full_like(rows, 1 << 30)
    for user in range(users + 1):
        bound = offsets_ref[0, user]
        begun = rows >= bound
        start = jnp.where(begun, bound, start)
        end = jnp.where(begun, end, jnp.minimum(end, bound))
    length = jnp.minimum(end - start, WINDOW)
    return jnp.maximum(start, rows - (WINDOW - 1)), lax.rsqrt(length.astype(jnp.float32))


def fill_weights(offsets_ref, users, first, rows, weights):
    span = (rows, rows)
    down = lax.broadcasted_iota(jnp.int32, span, 0)
    across = lax.broadcasted_iota(jnp.int32, span, 1)
    lo, scale = row_facts(offsets_ref, users, first + lax.broadcasted_iota(jnp.int32, (rows, 1), 0))
    for segment, shift in ((0, 0), (1, -2 * rows), (2, -rows)):
        key = first + shift + across
        mask = (key >= lo) & (key <= first + down)
        weights[0, segment] = jnp.where(mask, scale, 0.0)
    for segment, shift in ((0, 0), (1, 2 * rows), (2, rows)):
        query = first + shift + lax.broadcasted_iota(jnp.int32, (1, rows), 1)
        lo, scale = row_facts(offsets_ref, users, query)
        key = first + down
        mask = (key >= lo) & (key <= query)
        weights[1, segment] = jnp.where(mask, scale, 0.0)


def dot_nt(left, right):
    return lax.dot_general(left, right, (((1,), (1,)), ((), ())), preferred_element_type=jnp.float32)


def dot_nn(left, right):
    return jnp.dot(left, right, preferred_element_type=jnp.float32)


def kernel(
    size,
    heads,
    users,
    offsets_hbm,
    alpha_hbm,
    q_hbm,
    k_hbm,
    v_hbm,
    g_hbm,
    out_ref,
    dq_ref,
    dk_ref,
    dv_ref,
    sum_ref,
    offsets_ref,
    alpha_ref,
    own,
    far,
    near,
    da_ref,
    share,
    gathered,
    weights,
    raw_s,
    gw_s,
    w_s,
    gr_s,
    acc,
    load_sem,
    far_send,
    far_recv,
    near_send,
    near_recv,
    share_send,
    share_recv,
):
    rows = q_hbm.shape[1]
    coeff = 1.0 / math.sqrt(HEAD)
    me = lax.axis_index("ctx")
    core = lax.rem(me, 2)
    sibling = me + 1 - 2 * core
    ahead = lax.rem(me + 2, size)
    behind = lax.rem(me + size - 2, size)
    sources = ((k_hbm, v_hbm), (q_hbm, g_hbm))
    targets = (ahead, behind)
    results = ((out_ref, dq_ref), (dv_ref, dk_ref))

    def head_of(step, d):
        return lax.rem(step + d * (heads // 2), heads)

    def columns(head):
        return pl.ds(pl.multiple_of(head * HEAD, HEAD), HEAD)

    def far_copy(step, d, m):
        head = head_of(step, d)
        return pltpu.make_async_remote_copy(
            src_ref=sources[d][m].at[0, :, columns(head)],
            dst_ref=far.at[d, head, m],
            send_sem=far_send.at[d, head, m],
            recv_sem=far_recv.at[d, head, m],
            device_id={"ctx": targets[d]},
            device_id_type=MESH,
        )

    def near_copy(step, d, m, forwarded):
        head = head_of(step, d)
        source = far.at[d, head, m] if forwarded else sources[d][m].at[0, :, columns(head)]
        return pltpu.make_async_remote_copy(
            src_ref=source,
            dst_ref=near.at[d, head, m],
            send_sem=near_send.at[d, head, m],
            recv_sem=near_recv.at[d, head, m],
            device_id={"ctx": sibling},
            device_id_type=MESH,
        )

    rep = lax.axis_index("rep")
    pair_x = rep * 2 + core
    y, z = lax.rem(me // 2, LINE), me // (2 * LINE)
    places = (pair_x, y, z)

    def member(stage, n):
        if stage == 0:
            return {"ctx": me - core + lax.rem(n, 2), "rep": n // 2}
        return {"ctx": me + (n - places[stage]) * (2 if stage == 1 else 2 * LINE), "rep": rep}

    def share_copy(stage, hop, slot):
        return pltpu.make_async_remote_copy(
            src_ref=share.at[stage],
            dst_ref=gathered.at[stage, slot],
            send_sem=share_send.at[stage, hop],
            recv_sem=share_recv.at[stage, slot],
            device_id=member(stage, lax.rem(places[stage] + hop, LINE)),
            device_id_type=MESH,
        )

    def share_start(stage, value):
        share[stage] = value
        gathered[stage, places[stage]] = value
        for hop in range(1, LINE):
            share_copy(stage, hop, places[stage]).start()

    def share_finish(stage):
        for hop in range(1, LINE):
            share_copy(stage, hop, lax.rem(places[stage] + hop, LINE)).wait_recv()
        return jnp.sum(gathered[stage], axis=0)

    both = tuple((d, m) for d in range(2) for m in range(2))
    loads = [
        pltpu.make_async_copy(array.at[0], own.at[n], load_sem.at[n])
        for n, array in enumerate((q_hbm, g_hbm, k_hbm, v_hbm))
    ]
    facts = [
        pltpu.make_async_copy(offsets_hbm, offsets_ref, load_sem.at[4]),
        pltpu.make_async_copy(alpha_hbm, alpha_ref, load_sem.at[5]),
    ]
    for copy in facts:
        copy.start()
    barrier = pltpu.get_barrier_semaphore()
    for device in (ahead, behind, sibling):
        pl.semaphore_signal(barrier, inc=1, device_id={"ctx": device}, device_id_type=MESH)
    for stage in range(3):
        for hop in range(1, LINE):
            other = lax.rem(places[stage] + hop, LINE)
            pl.semaphore_signal(barrier, inc=1, device_id=member(stage, other), device_id_type=MESH)
    pl.semaphore_wait(barrier, 3 + 3 * (LINE - 1))

    for step in range(AHEAD):
        for d, m in both:
            far_copy(step, d, m).start()
    for copy in loads:
        copy.start()

    @pl.loop(0, heads)
    def _(step):
        for m in range(2):

            @pl.when(core == 0)
            def _():
                near_copy(step, 0, m, False).start()

            @pl.when(core == 1)
            def _():
                near_copy(step, 1, m, False).start()

    for copy in facts:
        copy.wait()
    fill_weights(offsets_ref, users, me * rows, rows, weights)
    lanes = lax.broadcasted_iota(jnp.int32, (STRIP, HEAD), 1)
    sublanes = lax.broadcasted_iota(jnp.int32, (STRIP, HEAD), 0)
    w_s[...] = jnp.zeros_like(w_s)
    gr_s[...] = jnp.zeros_like(gr_s)
    for copy in loads:
        copy.wait()

    def element(raw, gw, scale):
        half = raw * scale
        tanh = jnp.tanh(half)
        twice = 1.0 + tanh
        silu = half * twice
        return silu, gw * (twice + silu * (1.0 - tanh))

    def weigh(d, segment, at, silu, grad):
        weight = weights[d, segment, *at]
        w_s[d, segment, *at] = (silu * weight).astype(jnp.bfloat16)
        scaled = grad * weight
        gr_s[d, segment, *at] = scaled.astype(jnp.bfloat16)
        return scaled

    def fold(product):
        return jnp.sum(product.reshape(-1, 8, HEAD), axis=0)

    def own_rows(n, head):
        return own[n, :, columns(head)]

    middle = heads // 2 - 1

    @pl.loop(0, heads)
    def _(step):
        for d, m in both:
            far_copy(step, d, m).wait_recv()
        for m in range(2):

            @pl.when(core == 1)
            def _():
                near_copy(step, 0, m, True).start()

            @pl.when(core == 0)
            def _():
                near_copy(step, 1, m, True).start()

        @pl.when(step + AHEAD < heads)
        def _():
            for d, m in both:
                far_copy(step, d, m).wait_send()
            for d, m in both:
                far_copy(step + AHEAD, d, m).start()

        for stage in range(1, 3):

            @pl.when(step == middle + 1 + stage)
            def _():
                share_start(stage, share_finish(stage - 1))

        for d in range(2):
            head = head_of(step, d)
            r1, r2 = own_rows(2 * d, head), own_rows(2 * d + 1, head)
            raw_s[d, 0] = dot_nt(r1, own_rows(2 - 2 * d, head))
            raw_s[d, 1] = dot_nt(r1, far[d, head, 0])
            gw_s[d, 0] = dot_nt(r2, own_rows(3 - 2 * d, head))
            gw_s[d, 1] = dot_nt(r2, far[d, head, 1])
        for d in range(2):
            head = head_of(step, d)
            scale = 0.5 * coeff * alpha_ref[head]
            total = jnp.zeros((8, HEAD), jnp.float32)
            for row in range(0, rows, STRIP):
                for column in range(0, rows, HEAD):
                    at = (pl.ds(row, STRIP), pl.ds(column, HEAD))
                    if row // HEAD == column // HEAD:
                        gap = column - row + lanes - sublanes
                        mine = gap <= 0 if d == 0 else gap >= 0
                        raw = jnp.where(mine, raw_s[d, 0, *at], raw_s[d, 1, *at])
                        gw = jnp.where(mine, gw_s[d, 0, *at], gw_s[d, 1, *at])
                        silu, grad = element(raw, gw, scale)
                        total += fold((weigh(d, 0, at, silu, grad) + weigh(d, 1, at, silu, grad)) * raw)
                    else:
                        segment = int((row < column) == (d == 0))
                        raw = raw_s[d, segment, *at]
                        silu, grad = element(raw, gw_s[d, segment, *at], scale)
                        total += fold(weigh(d, segment, at, silu, grad) * raw)
            da_ref[d, step] = total * (0.5 * coeff)
            acc[d, 0] = dot_nn(w_s[d, 0], own_rows(3 - 2 * d, head)) + dot_nn(w_s[d, 1], far[d, head, 1])
            acc[d, 1] = dot_nn(gr_s[d, 0], own_rows(2 - 2 * d, head)) + dot_nn(gr_s[d, 1], far[d, head, 0])

        for d, m in both:
            near_copy(step, d, m, True).wait_recv()
        for d in range(2):
            head = head_of(step, d)
            raw_s[d, 2] = dot_nt(own_rows(2 * d, head), near[d, head, 0])
            gw_s[d, 2] = dot_nt(own_rows(2 * d + 1, head), near[d, head, 1])
        for d in range(2):
            head = head_of(step, d)
            scale = 0.5 * coeff * alpha_ref[head]
            total = jnp.zeros((8, HEAD), jnp.float32)
            for row in range(0, rows, STRIP):
                for column in range(0, rows, HEAD):
                    at = (pl.ds(row, STRIP), pl.ds(column, HEAD))
                    raw = raw_s[d, 2, *at]
                    silu, grad = element(raw, gw_s[d, 2, *at], scale)
                    total += fold(weigh(d, 2, at, silu, grad) * raw)
            da_ref[d, step] += total * (0.5 * coeff)
            first = acc[d, 0] + dot_nn(w_s[d, 2], near[d, head, 1])
            second = (acc[d, 1] + dot_nn(gr_s[d, 2], near[d, head, 0])) * scale
            results[d][0][0, :, columns(head)] = first.astype(jnp.bfloat16)
            results[d][1][0, :, columns(head)] = second.astype(jnp.bfloat16)

        @pl.when(step == middle)
        def _():
            for d in range(2):
                half = pl.ds(d * (heads // 2), heads // 2)
                share[0, half] = jnp.sum(da_ref[d, pl.ds(0, heads // 2)], axis=1)
            share_start(0, share[0])

    @pl.loop(0, heads)
    def _(step):
        for d, m in both:

            @pl.when(step + AHEAD >= heads)
            def _():
                far_copy(step, d, m).wait_send()

            near_copy(step, d, m, True).wait_send()

    sum_ref[...] = share_finish(2)
    for stage in range(3):
        for hop in range(1, LINE):
            share_copy(stage, hop, places[stage]).wait_send()


def shards(offsets, pairs, pair_count, queries, keys, values, cotangent, alpha):
    rows, width = queries.shape[1:]
    heads = alpha.shape[0]
    size = lax.axis_size("ctx")
    anywhere = pl.BlockSpec(memory_space=pl.ANY)

    def body(*refs):
        kernel(size, heads, offsets.shape[1] - 1, *refs)

    inputs = (offsets, alpha, queries, keys, values, cotangent)
    in_vmem = pltpu.VMEM((1, rows, width), jnp.bfloat16)
    *results, total = pl.pallas_call(
        body,
        out_shape=(in_vmem,) * 4 + (pltpu.VMEM((heads, HEAD), jnp.float32),),
        in_specs=[anywhere] * 6,
        out_specs=[pl.BlockSpec(memory_space=pltpu.VMEM)] * 5,
        scratch_shapes=[
            pltpu.SMEM(offsets.shape, jnp.int32),
            pltpu.SMEM(alpha.shape, jnp.float32),
            pltpu.VMEM((4, rows, width), jnp.bfloat16),
            pltpu.VMEM((2, heads, 2, rows, HEAD), jnp.bfloat16),
            pltpu.VMEM((2, heads, 2, rows, HEAD), jnp.bfloat16),
            pltpu.VMEM((2, heads, 8, HEAD), jnp.float32),
            pltpu.VMEM((3, heads, HEAD), jnp.float32),
            pltpu.VMEM((3, LINE, heads, HEAD), jnp.float32),
            pltpu.VMEM((2, 3, rows, rows), jnp.float32),
            pltpu.VMEM((2, 3, rows, rows), jnp.float32),
            pltpu.VMEM((2, 3, rows, rows), jnp.float32),
            pltpu.VMEM((2, 3, rows, rows), jnp.bfloat16),
            pltpu.VMEM((2, 3, rows, rows), jnp.bfloat16),
            pltpu.VMEM((2, 2, rows, HEAD), jnp.float32),
            pltpu.SemaphoreType.DMA((6,)),
            pltpu.SemaphoreType.DMA((2, heads, 2)),
            pltpu.SemaphoreType.DMA((2, heads, 2)),
            pltpu.SemaphoreType.DMA((2, heads, 2)),
            pltpu.SemaphoreType.DMA((2, heads, 2)),
            pltpu.SemaphoreType.DMA((3, LINE)),
            pltpu.SemaphoreType.DMA((3, LINE)),
        ],
        compiler_params=pltpu.CompilerParams(
            collective_id=0, has_side_effects=True, vmem_limit_bytes=40 * 1024 * 1024
        ),
        cost_estimate=pl.CostEstimate(
            flops=48 * heads * rows * rows * HEAD,
            bytes_accessed=8 * rows * width,
            transcendentals=4 * heads * rows * rows,
        ),
    )(*(pltpu.with_memory_space_constraint(array, pltpu.HBM) for array in inputs))
    return (*results, jnp.sum(total, axis=1))


def solution(mesh):
    return jax.shard_map(
        shards,
        mesh=mesh,
        in_specs=(
            P("rep", None),
            P("rep", "ctx", None),
            P("rep", "ctx"),
            P("rep", "ctx", None),
            P("rep", "ctx", None),
            P("rep", "ctx", None),
            P("rep", "ctx", None),
            P(),
        ),
        out_specs=(
            P("rep", "ctx", None),
            P("rep", "ctx", None),
            P("rep", "ctx", None),
            P("rep", "ctx", None),
            P(),
        ),
        check_vma=False,
    )
```

time: 404 us -> 51 us (0.13)
  blocking collectives: 218 us -> 0 us
  local copies, waits for them, and re-layouts: 101 us -> 3.17 us
  Pallas kernels: 0 us -> 46 us
  waiting for transfers between devices: 25.7 us -> 0 us
  loops' own time: 15.8 us -> 0 us
  matrix products: 14.3 us -> 0 us
  other arithmetic: 14.3 us -> 0.62 us
  starting transfers between devices: 11.3 us -> 0 us
    psum x1 -> x0, blocking collectives: 218 us -> none  [shards(): grad_alpha = lax.psum(da_acc, ('ctx', 'rep'))]
    dynamic_slice x140 -> x0, local copies, waits for them, and re-layouts: 64.8 us -> none  [the longest x56 28.4 us: add_block(): current = lax.dynamic_slice_in_dim(total, first, term.shape[0], 0)]
    pallas_call x0 -> x1, Pallas kernels: none -> 46 us  [shards(): pl.pallas_call(body, out_shape=(in_vmem,) * 4 + (pltpu.VMEM((heads, HEAD)...]
    ppermute x4 -> x0, waiting for transfers between devices: 25.7 us -> none  [from_behind(): return lax.ppermute(block, axis, route)]
    dynamic_update_slice x42 -> x0, local copies, waits for them, and re-layouts: 20.3 us -> none  [add_block(): return lax.dynamic_update_slice_in_dim(total, current + term, first, 0)]
    another operation x1 -> x0, loops' own time: 15.8 us -> none  [run_pairs(): return lax.fori_loop(0, count, one_pair, init)]
    dot_general x42 -> x0, matrix products: 14.3 us -> none  [the longest x7 4 us: tile_terms(): jnp.einsum('qhd,khd->hqk', shaped_g, shaped_v, preferred_element_type=jnp...]
    ppermute x4 -> x0, starting transfers between devices: 11.3 us -> none  [from_behind(): return lax.ppermute(block, axis, route)]
  transfers between devices with their start and end apart: 4 -> 0, of which waited for: 2 -> 0; matrix products, arithmetic and copies ran while one was open for 2% -> 0% of each run, Pallas kernels for 0% -> 0%
where the time goes in v1:
time: 51 us; the launch traced here: 50.4 us
  Pallas kernels  46 us (90%)
  local copies, waits for them, and re-layouts  3.17 us (6%)
  between operations  0.64 us (1%)
  other arithmetic  0.62 us (1%)
    pallas_call x1, Pallas kernels, shards(): pl.pallas_call(body, out_shape=(in_vmem,) * 4 + (pltpu.VMEM((heads, HEAD)...  46 us
    unnamed x4, local copies, waits for them, and re-layouts  3.17 us

profile of v1, /device:TPU:1, one launch (start us, length us, event | category | flops | bytes accessed | tf_op | source)
XLA Modules:
  0.0 50.4 jit_solution(3270117773374683272)
XLA Ops:
  0.6 46.0 %shard_map.101 = (bf16[1,256,1024]{2,1,0:T(8,128)(2,1)S(1)}, bf16[1,256,1024]{2,1,0:T(8,128)(2,1)S(1)}, bf16[1,256,1024]{2,1,0:T(8,128)(2,1)S(1)}, bf16[1,256,1024]{2,1,0:T(8,128)(2,1)S(1)}, f32[8,128]{1,0:T(8,128)S(1)}) custom-call(s32[1,17]{1,0:T(1,128)} %refs_0_.1, f32[8]{0:T(128)} %refs_1_.1, bf16[1,256,1024]{2,1,0:T(8,128)(2,1)} %refs_2_.1, ...), custom_call_target="tpu_custom_call" | custom-call | flops 3221225472 | bytes 2097152 | tf_op jit(solution)/shard_map/pallas_call | solution.py:346
  46.6 0.8 %copy.15 = bf16[1,256,1024]{2,1,0:T(8,128)(2,1)} copy(bf16[1,256,1024]{2,1,0:T(8,128)(2,1)S(1)} %get-tuple-element.15) | data formatting | bytes 1048576
  47.4 0.6 %reduce_sum.9 = f32[8]{0:T(128)} reduce(f32[8,128]{1,0:T(8,128)S(1)} %get-tuple-element.14, f32[]{:T(128)} %constant.0.clone.1), dimensions={1}, to_apply=%region_0.0 | reduce | flops 1016 | bytes 4132 | tf_op jit(solution)/shard_map/reduce_sum | solution.py:383
  48.0 0.8 %copy.16 = bf16[1,256,1024]{2,1,0:T(8,128)(2,1)} copy(bf16[1,256,1024]{2,1,0:T(8,128)(2,1)S(1)} %get-tuple-element.16) | data formatting | bytes 1048576
  48.8 0.8 %copy.17 = bf16[1,256,1024]{2,1,0:T(8,128)(2,1)} copy(bf16[1,256,1024]{2,1,0:T(8,128)(2,1)S(1)} %get-tuple-element.17) | data formatting | bytes 1048576
  49.6 0.8 %copy.18 = bf16[1,256,1024]{2,1,0:T(8,128)(2,1)} copy(bf16[1,256,1024]{2,1,0:T(8,128)(2,1)S(1)} %get-tuple-element.18) | data formatting | bytes 1048576

commit v2 on v1

--- a/solution.py
+++ b/solution.py
@@ -10,7 +10,7 @@
 WINDOW = 512
 HEAD = 128
 STRIP = 32
-AHEAD = 4
+AHEAD = 2
 LINE = 8
 MESH = pl.DeviceIdType.MESH
 
@@ -88,16 +88,22 @@
     near_recv,
     share_send,
     share_recv,
+    reached,
 ):
     rows = q_hbm.shape[1]
     coeff = 1.0 / math.sqrt(HEAD)
     me = lax.axis_index("ctx")
     core = lax.rem(me, 2)
     sibling = me + 1 - 2 * core
-    ahead = lax.rem(me + 2, size)
-    behind = lax.rem(me + size - 2, size)
+    ahead, behind = jnp.minimum(me + 2, size - 1), jnp.maximum(me - 2, 0)
+    has_ahead, has_behind = me < size - 2, me >= 2
     sources = ((k_hbm, v_hbm), (q_hbm, g_hbm))
     targets = (ahead, behind)
+    sends, receives = (has_ahead, has_behind), (has_behind, has_ahead)
+    direct = (core == 0, core == 1)
+    relays = ((core == 1) & has_behind, (core == 0) & has_ahead)
+    near_sends = (me != 1, me != size - 2)
+    near_receives = (me != 0, me != size - 1)
     results = ((out_ref, dq_ref), (dv_ref, dk_ref))
 
     def head_of(step, d):
@@ -160,7 +166,6 @@
             share_copy(stage, hop, lax.rem(places[stage] + hop, LINE)).wait_recv()
         return jnp.sum(gathered[stage], axis=0)
 
-    both = tuple((d, m) for d in range(2) for m in range(2))
     loads = [
         pltpu.make_async_copy(array.at[0], own.at[n], load_sem.at[n])
         for n, array in enumerate((q_hbm, g_hbm, k_hbm, v_hbm))
@@ -171,32 +176,79 @@
     ]
     for copy in facts:
         copy.start()
+    def far_start(step):
+        for d in range(2):
+
+            @pl.when(sends[d])
+            def _():
+                for m in range(2):
+                    far_copy(step, d, m).start()
+
+    def near_start(step, conditions, forwarded):
+        for d in range(2):
+
+            @pl.when(conditions[d])
+            def _():
+                for m in range(2):
+                    near_copy(step, d, m, forwarded).start()
+
+    def wait_if(condition, *waits):
+        @pl.when(condition)
+        def _():
+            for wait in waits:
+                wait()
+
     barrier = pltpu.get_barrier_semaphore()
-    for device in (ahead, behind, sibling):
-        pl.semaphore_signal(barrier, inc=1, device_id={"ctx": device}, device_id_type=MESH)
-    for stage in range(3):
+
+    def along_z(distance):
+        inside = z + distance < LINE if distance > 0 else z + distance >= 0
+        return inside, {"ctx": jnp.clip(me + 2 * LINE * distance, 0, size - 1)}
+
+    def count(conditions):
+        return sum(condition.astype(jnp.int32) for condition in conditions)
+
+    greeted = [(has_ahead, {"ctx": ahead}), (has_behind, {"ctx": behind}), along_z(1), along_z(-1)]
+    for exists, device in greeted:
+
+        @pl.when(exists)
+        def _():
+            pl.semaphore_signal(barrier, inc=1, device_id=device, device_id_type=MESH)
+
+    pl.semaphore_signal(barrier, inc=1, device_id={"ctx": sibling}, device_id_type=MESH)
+    for stage in range(2):
         for hop in range(1, LINE):
             other = lax.rem(places[stage] + hop, LINE)
             pl.semaphore_signal(barrier, inc=1, device_id=member(stage, other), device_id_type=MESH)
-    pl.semaphore_wait(barrier, 3 + 3 * (LINE - 1))
+    pl.semaphore_wait(barrier, 1 + 2 * (LINE - 1) + count([exists for exists, _ in greeted]))
 
     for step in range(AHEAD):
-        for d, m in both:
-            far_copy(step, d, m).start()
+        far_start(step)
     for copy in loads:
         copy.start()
-
-    @pl.loop(0, heads)
-    def _(step):
-        for m in range(2):
-
-            @pl.when(core == 0)
+    for step in range(AHEAD):
+        near_start(step, direct, False)
+
+    def pass_on(n):
+        for distance in (1 << n, -(1 << n)):
+            exists, device = along_z(distance)
+
+            @pl.when(exists)
             def _():
-                near_copy(step, 0, m, False).start()
-
-            @pl.when(core == 1)
-            def _():
-                near_copy(step, 1, m, False).start()
+                pl.semaphore_signal(reached.at[n], inc=1, device_id=device, device_id_type=MESH)
+
+    def learn(n):
+        pl.semaphore_wait(reached.at[n], count([along_z(1 << n)[0], along_z(-(1 << n))[0]]))
+
+    pass_on(0)
+    for d in range(2):
+
+        @pl.when(jnp.logical_not(receives[d]))
+        def _():
+            far[d] = jnp.zeros(far.shape[1:], far.dtype)
+
+        @pl.when(jnp.logical_not(near_receives[d]))
+        def _():
+            near[d] = jnp.zeros(near.shape[1:], near.dtype)
 
     for copy in facts:
         copy.wait()
@@ -213,7 +265,7 @@
         tanh = jnp.tanh(half)
         twice = 1.0 + tanh
         silu = half * twice
-        return silu, gw * (twice + silu * (1.0 - tanh))
+        return silu, gw * scale * (twice + silu * (1.0 - tanh))
 
     def weigh(d, segment, at, silu, grad):
         weight = weights[d, segment, *at]
@@ -232,29 +284,30 @@
 
     @pl.loop(0, heads)
     def _(step):
-        for d, m in both:
-            far_copy(step, d, m).wait_recv()
-        for m in range(2):
-
-            @pl.when(core == 1)
+        for d in range(2):
+            wait_if(receives[d], *(far_copy(step, d, m).wait_recv for m in range(2)))
+        near_start(step, relays, True)
+
+        @pl.when(step + AHEAD < heads)
+        def _():
+            for d in range(2):
+                wait_if(sends[d], *(far_copy(step, d, m).wait_send for m in range(2)))
+            far_start(step + AHEAD)
+            near_start(step + AHEAD, direct, False)
+
+        for n in range(2):
+
+            @pl.when(step == 2 * n + 2)
             def _():
-                near_copy(step, 0, m, True).start()
-
-            @pl.when(core == 0)
+                learn(n)
+                pass_on(n + 1)
+
+        for stage in range(1, 3):
+
+            @pl.when(step == heads - 3 + stage)
             def _():
-                near_copy(step, 1, m, True).start()
-
-        @pl.when(step + AHEAD < heads)
-        def _():
-            for d, m in both:
-                far_copy(step, d, m).wait_send()
-            for d, m in both:
-                far_copy(step + AHEAD, d, m).start()
-
-        for stage in range(1, 3):
-
-            @pl.when(step == middle + 1 + stage)
-            def _():
+                if stage == 2:
+                    learn(2)
                 share_start(stage, share_finish(stage - 1))
 
         for d in range(2):
@@ -283,12 +336,12 @@
                         raw = raw_s[d, segment, *at]
                         silu, grad = element(raw, gw_s[d, segment, *at], scale)
                         total += fold(weigh(d, segment, at, silu, grad) * raw)
-            da_ref[d, step] = total * (0.5 * coeff)
+            da_ref[d, step] = total / alpha_ref[head]
             acc[d, 0] = dot_nn(w_s[d, 0], own_rows(3 - 2 * d, head)) + dot_nn(w_s[d, 1], far[d, head, 1])
             acc[d, 1] = dot_nn(gr_s[d, 0], own_rows(2 - 2 * d, head)) + dot_nn(gr_s[d, 1], far[d, head, 0])
 
-        for d, m in both:
-            near_copy(step, d, m, True).wait_recv()
+        for d in range(2):
+            wait_if(near_receives[d], *(near_copy(step, d, m, True).wait_recv for m in range(2)))
         for d in range(2):
             head = head_of(step, d)
             raw_s[d, 2] = dot_nt(own_rows(2 * d, head), near[d, head, 0])
@@ -303,9 +356,9 @@
                     raw = raw_s[d, 2, *at]
                     silu, grad = element(raw, gw_s[d, 2, *at], scale)
                     total += fold(weigh(d, 2, at, silu, grad) * raw)
-            da_ref[d, step] += total * (0.5 * coeff)
+            da_ref[d, step] += total / alpha_ref[head]
             first = acc[d, 0] + dot_nn(w_s[d, 2], near[d, head, 1])
-            second = (acc[d, 1] + dot_nn(gr_s[d, 2], near[d, head, 0])) * scale
+            second = acc[d, 1] + dot_nn(gr_s[d, 2], near[d, head, 0])
             results[d][0][0, :, columns(head)] = first.astype(jnp.bfloat16)
             results[d][1][0, :, columns(head)] = second.astype(jnp.bfloat16)
 
@@ -318,13 +371,11 @@
 
     @pl.loop(0, heads)
     def _(step):
-        for d, m in both:
-
-            @pl.when(step + AHEAD >= heads)
-            def _():
-                far_copy(step, d, m).wait_send()
-
-            near_copy(step, d, m, True).wait_send()
+        for d in range(2):
+            wait_if(
+                sends[d] & (step + AHEAD >= heads), *(far_copy(step, d, m).wait_send for m in range(2))
+            )
+            wait_if(near_sends[d], *(near_copy(step, d, m, True).wait_send for m in range(2)))
 
     sum_ref[...] = share_finish(2)
     for stage in range(3):
@@ -370,6 +421,7 @@
             pltpu.SemaphoreType.DMA((2, heads, 2)),
             pltpu.SemaphoreType.DMA((3, LINE)),
             pltpu.SemaphoreType.DMA((3, LINE)),
+            pltpu.SemaphoreType.REGULAR((3,)),
         ],
         compiler_params=pltpu.CompilerParams(
             collective_id=0, has_side_effects=True, vmem_limit_bytes=40 * 1024 * 1024

time: 51 us -> 52 us (1.020)
  the two profiles are of different devices: /device:TPU:1 before, /device:TPU:2 now
where the time goes in v2:
time: 52 us; the launch traced here: 51.8 us
  Pallas kernels  47.4 us (91%)
  local copies, waits for them, and re-layouts  3.17 us (6%)
  between operations  0.64 us (1%)
  other arithmetic  0.62 us (1%)
    pallas_call x1, Pallas kernels, shards(): pl.pallas_call(body, out_shape=(in_vmem,) * 4 + (pltpu.VMEM((heads, HEAD)...  47.4 us
    unnamed x4, local copies, waits for them, and re-layouts  3.17 us

profile of v2, /device:TPU:2, one launch (start us, length us, event | category | flops | bytes accessed | tf_op | source)
XLA Modules:
  0.0 51.8 jit_solution(16005077060346476930)
XLA Ops:
  0.6 47.4 %shard_map.101 = (bf16[1,256,1024]{2,1,0:T(8,128)(2,1)S(1)}, bf16[1,256,1024]{2,1,0:T(8,128)(2,1)S(1)}, bf16[1,256,1024]{2,1,0:T(8,128)(2,1)S(1)}, bf16[1,256,1024]{2,1,0:T(8,128)(2,1)S(1)}, f32[8,128]{1,0:T(8,128)S(1)}) custom-call(s32[1,17]{1,0:T(1,128)} %refs_0_.1, f32[8]{0:T(128)} %refs_1_.1, bf16[1,256,1024]{2,1,0:T(8,128)(2,1)} %refs_2_.1, ...), custom_call_target="tpu_custom_call" | custom-call | flops 3221225472 | bytes 2097152 | tf_op jit(solution)/shard_map/pallas_call | solution.py:397
  48.0 0.8 %copy.15 = bf16[1,256,1024]{2,1,0:T(8,128)(2,1)} copy(bf16[1,256,1024]{2,1,0:T(8,128)(2,1)S(1)} %get-tuple-element.15) | data formatting | bytes 1048576
  48.8 0.6 %reduce_sum.9 = f32[8]{0:T(128)} reduce(f32[8,128]{1,0:T(8,128)S(1)} %get-tuple-element.14, f32[]{:T(128)} %constant.0.clone.1), dimensions={1}, to_apply=%region_0.0 | reduce | flops 1016 | bytes 4132 | tf_op jit(solution)/shard_map/reduce_sum | solution.py:435
  49.5 0.8 %copy.16 = bf16[1,256,1024]{2,1,0:T(8,128)(2,1)} copy(bf16[1,256,1024]{2,1,0:T(8,128)(2,1)S(1)} %get-tuple-element.16) | data formatting | bytes 1048576
  50.2 0.8 %copy.17 = bf16[1,256,1024]{2,1,0:T(8,128)(2,1)} copy(bf16[1,256,1024]{2,1,0:T(8,128)(2,1)S(1)} %get-tuple-element.17) | data formatting | bytes 1048576
  51.0 0.8 %copy.18 = bf16[1,256,1024]{2,1,0:T(8,128)(2,1)} copy(bf16[1,256,1024]{2,1,0:T(8,128)(2,1)S(1)} %get-tuple-element.18) | data formatting | bytes 1048576

commit v3 on v2

--- a/solution.py
+++ b/solution.py
@@ -10,7 +10,7 @@
 WINDOW = 512
 HEAD = 128
 STRIP = 32
-AHEAD = 2
+AHEAD = 3
 LINE = 8
 MESH = pl.DeviceIdType.MESH
 
@@ -82,6 +82,7 @@
     gr_s,
     acc,
     load_sem,
+    fact_sem,
     far_send,
     far_recv,
     near_send,
@@ -97,7 +98,7 @@
     sibling = me + 1 - 2 * core
     ahead, behind = jnp.minimum(me + 2, size - 1), jnp.maximum(me - 2, 0)
     has_ahead, has_behind = me < size - 2, me >= 2
-    sources = ((k_hbm, v_hbm), (q_hbm, g_hbm))
+    arrays = (q_hbm, g_hbm, k_hbm, v_hbm)
     targets = (ahead, behind)
     sends, receives = (has_ahead, has_behind), (has_behind, has_ahead)
     direct = (core == 0, core == 1)
@@ -115,7 +116,7 @@
     def far_copy(step, d, m):
         head = head_of(step, d)
         return pltpu.make_async_remote_copy(
-            src_ref=sources[d][m].at[0, :, columns(head)],
+            src_ref=own.at[2 - 2 * d + m, :, columns(head)],
             dst_ref=far.at[d, head, m],
             send_sem=far_send.at[d, head, m],
             recv_sem=far_recv.at[d, head, m],
@@ -125,7 +126,7 @@
 
     def near_copy(step, d, m, forwarded):
         head = head_of(step, d)
-        source = far.at[d, head, m] if forwarded else sources[d][m].at[0, :, columns(head)]
+        source = far.at[d, head, m] if forwarded else own.at[2 - 2 * d + m, :, columns(head)]
         return pltpu.make_async_remote_copy(
             src_ref=source,
             dst_ref=near.at[d, head, m],
@@ -166,14 +167,24 @@
             share_copy(stage, hop, lax.rem(places[stage] + hop, LINE)).wait_recv()
         return jnp.sum(gathered[stage], axis=0)
 
-    loads = [
-        pltpu.make_async_copy(array.at[0], own.at[n], load_sem.at[n])
-        for n, array in enumerate((q_hbm, g_hbm, k_hbm, v_hbm))
+    def load(n, head):
+        return pltpu.make_async_copy(
+            arrays[n].at[0, :, columns(head)], own.at[n, :, columns(head)], load_sem.at[n, head]
+        )
+
+    def sent_at(step):
+        return [(2 - 2 * d + m, head_of(step, d)) for d in range(2) for m in range(2)]
+
+    facts = [
+        pltpu.make_async_copy(offsets_hbm, offsets_ref, fact_sem.at[0]),
+        pltpu.make_async_copy(alpha_hbm, alpha_ref, fact_sem.at[1]),
     ]
-    facts = [
-        pltpu.make_async_copy(offsets_hbm, offsets_ref, load_sem.at[4]),
-        pltpu.make_async_copy(alpha_hbm, alpha_ref, load_sem.at[5]),
-    ]
+
+    @pl.loop(0, heads)
+    def _(step):
+        for piece in sent_at(step):
+            load(*piece).start()
+
     for copy in facts:
         copy.start()
     def far_start(step):
@@ -222,9 +233,9 @@
     pl.semaphore_wait(barrier, 1 + 2 * (LINE - 1) + count([exists for exists, _ in greeted]))
 
     for step in range(AHEAD):
+        for piece in sent_at(step):
+            load(*piece).wait()
         far_start(step)
-    for copy in loads:
-        copy.start()
     for step in range(AHEAD):
         near_start(step, direct, False)
 
@@ -257,8 +268,10 @@
     sublanes = lax.broadcasted_iota(jnp.int32, (STRIP, HEAD), 0)
     w_s[...] = jnp.zeros_like(w_s)
     gr_s[...] = jnp.zeros_like(gr_s)
-    for copy in loads:
-        copy.wait()
+    @pl.loop(AHEAD, heads)
+    def _(step):
+        for piece in sent_at(step):
+            load(*piece).wait()
 
     def element(raw, gw, scale):
         half = raw * scale
@@ -304,7 +317,7 @@
 
         for stage in range(1, 3):
 
-            @pl.when(step == heads - 3 + stage)
+            @pl.when(step == middle + 1 + stage)
             def _():
                 if stage == 2:
                     learn(2)
@@ -414,7 +427,8 @@
             pltpu.VMEM((2, 3, rows, rows), jnp.bfloat16),
             pltpu.VMEM((2, 3, rows, rows), jnp.bfloat16),
             pltpu.VMEM((2, 2, rows, HEAD), jnp.float32),
-            pltpu.SemaphoreType.DMA((6,)),
+            pltpu.SemaphoreType.DMA((4, heads)),
+            pltpu.SemaphoreType.DMA((2,)),
             pltpu.SemaphoreType.DMA((2, heads, 2)),
             pltpu.SemaphoreType.DMA((2, heads, 2)),
             pltpu.SemaphoreType.DMA((2, heads, 2)),

time: 52 us -> 50.9 us (0.979)
  the two profiles are of different devices: /device:TPU:2 before, /device:TPU:1 now
where the time goes in v3:
time: 50.9 us; the launch traced here: 50.7 us
  Pallas kernels  46.2 us (91%)
  local copies, waits for them, and re-layouts  3.17 us (6%)
  between operations  0.64 us (1%)
  other arithmetic  0.62 us (1%)
    pallas_call x1, Pallas kernels, shards(): pl.pallas_call(body, out_shape=(in_vmem,) * 4 + (pltpu.VMEM((heads, HEAD)...  46.2 us
    unnamed x4, local copies, waits for them, and re-layouts  3.17 us

profile of v3, /device:TPU:1, one launch (start us, length us, event | category | flops | bytes accessed | tf_op | source)
XLA Modules:
  0.0 50.7 jit_solution(12089515417562543854)
XLA Ops:
  0.6 46.2 %shard_map.101 = (bf16[1,256,1024]{2,1,0:T(8,128)(2,1)S(1)}, bf16[1,256,1024]{2,1,0:T(8,128)(2,1)S(1)}, bf16[1,256,1024]{2,1,0:T(8,128)(2,1)S(1)}, bf16[1,256,1024]{2,1,0:T(8,128)(2,1)S(1)}, f32[8,128]{1,0:T(8,128)S(1)}) custom-call(s32[1,17]{1,0:T(1,128)} %refs_0_.1, f32[8]{0:T(128)} %refs_1_.1, bf16[1,256,1024]{2,1,0:T(8,128)(2,1)} %refs_2_.1, ...), custom_call_target="tpu_custom_call" | custom-call | flops 3221225472 | bytes 2097152 | tf_op jit(solution)/shard_map/pallas_call | solution.py:410
  46.9 0.8 %copy.15 = bf16[1,256,1024]{2,1,0:T(8,128)(2,1)} copy(bf16[1,256,1024]{2,1,0:T(8,128)(2,1)S(1)} %get-tuple-element.15) | data formatting | bytes 1048576
  47.7 0.6 %reduce_sum.9 = f32[8]{0:T(128)} reduce(f32[8,128]{1,0:T(8,128)S(1)} %get-tuple-element.14, f32[]{:T(128)} %constant.0.clone.1), dimensions={1}, to_apply=%region_0.0 | reduce | flops 1016 | bytes 4132 | tf_op jit(solution)/shard_map/reduce_sum | solution.py:449
  48.3 0.8 %copy.16 = bf16[1,256,1024]{2,1,0:T(8,128)(2,1)} copy(bf16[1,256,1024]{2,1,0:T(8,128)(2,1)S(1)} %get-tuple-element.16) | data formatting | bytes 1048576
  49.1 0.8 %copy.17 = bf16[1,256,1024]{2,1,0:T(8,128)(2,1)} copy(bf16[1,256,1024]{2,1,0:T(8,128)(2,1)S(1)} %get-tuple-element.17) | data formatting | bytes 1048576
  49.9 0.8 %copy.18 = bf16[1,256,1024]{2,1,0:T(8,128)(2,1)} copy(bf16[1,256,1024]{2,1,0:T(8,128)(2,1)S(1)} %get-tuple-element.18) | data formatting | bytes 1048576

commit v4 on v3

--- a/solution.py
+++ b/solution.py
@@ -10,7 +10,7 @@
 WINDOW = 512
 HEAD = 128
 STRIP = 32
-AHEAD = 3
+AHEAD = 2
 LINE = 8
 MESH = pl.DeviceIdType.MESH
 
@@ -295,18 +295,21 @@
 
     middle = heads // 2 - 1
 
+    def send_next(step):
+        for d in range(2):
+            wait_if(sends[d], *(far_copy(step, d, m).wait_send for m in range(2)))
+        far_start(step + AHEAD)
+        near_start(step + AHEAD, direct, False)
+
     @pl.loop(0, heads)
     def _(step):
         for d in range(2):
             wait_if(receives[d], *(far_copy(step, d, m).wait_recv for m in range(2)))
         near_start(step, relays, True)
 
-        @pl.when(step + AHEAD < heads)
-        def _():
-            for d in range(2):
-                wait_if(sends[d], *(far_copy(step, d, m).wait_send for m in range(2)))
-            far_start(step + AHEAD)
-            near_start(step + AHEAD, direct, False)
+        @pl.when(step < middle)
+        def _():
+            send_next(step)
 
         for n in range(2):
 
@@ -314,14 +317,6 @@
             def _():
                 learn(n)
                 pass_on(n + 1)
-
-        for stage in range(1, 3):
-
-            @pl.when(step == middle + 1 + stage)
-            def _():
-                if stage == 2:
-                    learn(2)
-                share_start(stage, share_finish(stage - 1))
 
         for d in range(2):
             head = head_of(step, d)
@@ -353,6 +348,15 @@
             acc[d, 0] = dot_nn(w_s[d, 0], own_rows(3 - 2 * d, head)) + dot_nn(w_s[d, 1], far[d, head, 1])
             acc[d, 1] = dot_nn(gr_s[d, 0], own_rows(2 - 2 * d, head)) + dot_nn(gr_s[d, 1], far[d, head, 0])
 
+        for stage in range(1, 3):
+
+            @pl.when(step == middle + stage)
+            def _():
+                if stage == 2:
+                    learn(2)
+                share_start(stage, share_finish(stage - 1))
+                send_next(step)
+
         for d in range(2):
             wait_if(near_receives[d], *(near_copy(step, d, m, True).wait_recv for m in range(2)))
         for d in range(2):
@@ -381,6 +385,7 @@
                 half = pl.ds(d * (heads // 2), heads // 2)
                 share[0, half] = jnp.sum(da_ref[d, pl.ds(0, heads // 2)], axis=1)
             share_start(0, share[0])
+            send_next(step)
 
     @pl.loop(0, heads)
     def _(step):

time: 50.9 us -> 53.2 us (1.045)
  Pallas kernels: 46.2 us -> 48.6 us
    pallas_call x1, Pallas kernels: 46.2 us -> 48.6 us  [shards(): pl.pallas_call(body, out_shape=(in_vmem,) * 4 + (pltpu.VMEM((heads, HEAD)...]
where the time goes in v4:
time: 53.2 us; the launch traced here: 53 us
  Pallas kernels  48.6 us (91%)
  local copies, waits for them, and re-layouts  3.17 us (6%)
  between operations  0.64 us (1%)
  other arithmetic  0.62 us (1%)
    pallas_call x1, Pallas kernels, shards(): pl.pallas_call(body, out_shape=(in_vmem,) * 4 + (pltpu.VMEM((heads, HEAD)...  48.6 us
    unnamed x4, local copies, waits for them, and re-layouts  3.17 us

profile of v4, /device:TPU:1, one launch (start us, length us, event | category | flops | bytes accessed | tf_op | source)
XLA Modules:
  0.0 53.0 jit_solution(15518065425801523700)
XLA Ops:
  0.6 48.6 %shard_map.101 = (bf16[1,256,1024]{2,1,0:T(8,128)(2,1)S(1)}, bf16[1,256,1024]{2,1,0:T(8,128)(2,1)S(1)}, bf16[1,256,1024]{2,1,0:T(8,128)(2,1)S(1)}, bf16[1,256,1024]{2,1,0:T(8,128)(2,1)S(1)}, f32[8,128]{1,0:T(8,128)S(1)}) custom-call(s32[1,17]{1,0:T(1,128)} %refs_0_.1, f32[8]{0:T(128)} %refs_1_.1, bf16[1,256,1024]{2,1,0:T(8,128)(2,1)} %refs_2_.1, ...), custom_call_target="tpu_custom_call" | custom-call | flops 3221225472 | bytes 2097152 | tf_op jit(solution)/shard_map/pallas_call | solution.py:415
  49.2 0.8 %copy.15 = bf16[1,256,1024]{2,1,0:T(8,128)(2,1)} copy(bf16[1,256,1024]{2,1,0:T(8,128)(2,1)S(1)} %get-tuple-element.15) | data formatting | bytes 1048576
  50.0 0.6 %reduce_sum.9 = f32[8]{0:T(128)} reduce(f32[8,128]{1,0:T(8,128)S(1)} %get-tuple-element.14, f32[]{:T(128)} %constant.0.clone.1), dimensions={1}, to_apply=%region_0.0 | reduce | flops 1016 | bytes 4132 | tf_op jit(solution)/shard_map/reduce_sum | solution.py:454
  50.6 0.8 %copy.16 = bf16[1,256,1024]{2,1,0:T(8,128)(2,1)} copy(bf16[1,256,1024]{2,1,0:T(8,128)(2,1)S(1)} %get-tuple-element.16) | data formatting | bytes 1048576
  51.4 0.8 %copy.17 = bf16[1,256,1024]{2,1,0:T(8,128)(2,1)} copy(bf16[1,256,1024]{2,1,0:T(8,128)(2,1)S(1)} %get-tuple-element.17) | data formatting | bytes 1048576
  52.2 0.8 %copy.18 = bf16[1,256,1024]{2,1,0:T(8,128)(2,1)} copy(bf16[1,256,1024]{2,1,0:T(8,128)(2,1)S(1)} %get-tuple-element.18) | data formatting | bytes 1048576

commit v5 on v3

--- a/solution.py
+++ b/solution.py
@@ -188,12 +188,13 @@
     for copy in facts:
         copy.start()
     def far_start(step):
-        for d in range(2):
-
-            @pl.when(sends[d])
-            def _():
-                for m in range(2):
-                    far_copy(step, d, m).start()
+        for first in range(2):
+            for m in range(2):
+                for d in (first, 1 - first):
+
+                    @pl.when((core == first) & sends[d])
+                    def _():
+                        far_copy(step, d, m).start()
 
     def near_start(step, conditions, forwarded):
         for d in range(2):

time: 50.9 us -> 50.9 us (level)
  no operation moved by 1% of the time
where the time goes in v5:
time: 50.9 us; the launch traced here: 50.7 us
  Pallas kernels  46.2 us (91%)
  local copies, waits for them, and re-layouts  3.17 us (6%)
  between operations  0.64 us (1%)
  other arithmetic  0.62 us (1%)
    pallas_call x1, Pallas kernels, shards(): pl.pallas_call(body, out_shape=(in_vmem,) * 4 + (pltpu.VMEM((heads, HEAD)...  46.2 us
    unnamed x4, local copies, waits for them, and re-layouts  3.17 us

profile of v5, /device:TPU:1, one launch (start us, length us, event | category | flops | bytes accessed | tf_op | source)
XLA Modules:
  0.0 50.7 jit_solution(15750709877605301717)
XLA Ops:
  0.6 46.2 %shard_map.101 = (bf16[1,256,1024]{2,1,0:T(8,128)(2,1)S(1)}, bf16[1,256,1024]{2,1,0:T(8,128)(2,1)S(1)}, bf16[1,256,1024]{2,1,0:T(8,128)(2,1)S(1)}, bf16[1,256,1024]{2,1,0:T(8,128)(2,1)S(1)}, f32[8,128]{1,0:T(8,128)S(1)}) custom-call(s32[1,17]{1,0:T(1,128)} %refs_0_.1, f32[8]{0:T(128)} %refs_1_.1, bf16[1,256,1024]{2,1,0:T(8,128)(2,1)} %refs_2_.1, ...), custom_call_target="tpu_custom_call" | custom-call | flops 3221225472 | bytes 2097152 | tf_op jit(solution)/shard_map/pallas_call | solution.py:411
  46.9 0.8 %copy.15 = bf16[1,256,1024]{2,1,0:T(8,128)(2,1)} copy(bf16[1,256,1024]{2,1,0:T(8,128)(2,1)S(1)} %get-tuple-element.15) | data formatting | bytes 1048576
  47.7 0.6 %reduce_sum.9 = f32[8]{0:T(128)} reduce(f32[8,128]{1,0:T(8,128)S(1)} %get-tuple-element.14, f32[]{:T(128)} %constant.0.clone.1), dimensions={1}, to_apply=%region_0.0 | reduce | flops 1016 | bytes 4132 | tf_op jit(solution)/shard_map/reduce_sum | solution.py:450
  48.3 0.8 %copy.16 = bf16[1,256,1024]{2,1,0:T(8,128)(2,1)} copy(bf16[1,256,1024]{2,1,0:T(8,128)(2,1)S(1)} %get-tuple-element.16) | data formatting | bytes 1048576
  49.1 0.8 %copy.17 = bf16[1,256,1024]{2,1,0:T(8,128)(2,1)} copy(bf16[1,256,1024]{2,1,0:T(8,128)(2,1)S(1)} %get-tuple-element.17) | data formatting | bytes 1048576
  49.9 0.8 %copy.18 = bf16[1,256,1024]{2,1,0:T(8,128)(2,1)} copy(bf16[1,256,1024]{2,1,0:T(8,128)(2,1)S(1)} %get-tuple-element.18) | data formatting | bytes 1048576

commit v6 on v5

--- a/solution.py
+++ b/solution.py
@@ -296,18 +296,21 @@
 
     middle = heads // 2 - 1
 
+    def send_next(step):
+        for d in range(2):
+            wait_if(sends[d], *(far_copy(step, d, m).wait_send for m in range(2)))
+        far_start(step + AHEAD)
+        near_start(step + AHEAD, direct, False)
+
     @pl.loop(0, heads)
     def _(step):
         for d in range(2):
             wait_if(receives[d], *(far_copy(step, d, m).wait_recv for m in range(2)))
         near_start(step, relays, True)
 
-        @pl.when(step + AHEAD < heads)
-        def _():
-            for d in range(2):
-                wait_if(sends[d], *(far_copy(step, d, m).wait_send for m in range(2)))
-            far_start(step + AHEAD)
-            near_start(step + AHEAD, direct, False)
+        @pl.when(step < middle)
+        def _():
+            send_next(step)
 
         for n in range(2):
 
@@ -323,6 +326,8 @@
                 if stage == 2:
                     learn(2)
                 share_start(stage, share_finish(stage - 1))
+                if stage == 2:
+                    send_next(heads - 1 - AHEAD)
 
         for d in range(2):
             head = head_of(step, d)
@@ -382,6 +387,7 @@
                 half = pl.ds(d * (heads // 2), heads // 2)
                 share[0, half] = jnp.sum(da_ref[d, pl.ds(0, heads // 2)], axis=1)
             share_start(0, share[0])
+            send_next(middle)
 
     @pl.loop(0, heads)
     def _(step):

time: 50.9 us -> 50.5 us (level)
  the two profiles are of different devices: /device:TPU:1 before, /device:TPU:6 now
where the time goes in v6:
time: 50.5 us; the launch traced here: 50.3 us
  Pallas kernels  45.9 us (91%)
  local copies, waits for them, and re-layouts  3.17 us (6%)
  between operations  0.64 us (1%)
  other arithmetic  0.62 us (1%)
    pallas_call x1, Pallas kernels, shards(): pl.pallas_call(body, out_shape=(in_vmem,) * 4 + (pltpu.VMEM((heads, HEAD)...  45.9 us
    unnamed x4, local copies, waits for them, and re-layouts  3.17 us

profile of v6, /device:TPU:6, one launch (start us, length us, event | category | flops | bytes accessed | tf_op | source)
XLA Modules:
  0.0 50.3 jit_solution(9270211450771223508)
XLA Ops:
  0.6 45.9 %shard_map.101 = (bf16[1,256,1024]{2,1,0:T(8,128)(2,1)S(1)}, bf16[1,256,1024]{2,1,0:T(8,128)(2,1)S(1)}, bf16[1,256,1024]{2,1,0:T(8,128)(2,1)S(1)}, bf16[1,256,1024]{2,1,0:T(8,128)(2,1)S(1)}, f32[8,128]{1,0:T(8,128)S(1)}) custom-call(s32[1,17]{1,0:T(1,128)} %refs_0_.1, f32[8]{0:T(128)} %refs_1_.1, bf16[1,256,1024]{2,1,0:T(8,128)(2,1)} %refs_2_.1, ...), custom_call_target="tpu_custom_call" | custom-call | flops 3221225472 | bytes 2097152 | tf_op jit(solution)/shard_map/pallas_call | solution.py:417
  46.5 0.8 %copy.15 = bf16[1,256,1024]{2,1,0:T(8,128)(2,1)} copy(bf16[1,256,1024]{2,1,0:T(8,128)(2,1)S(1)} %get-tuple-element.15) | data formatting | bytes 1048576
  47.3 0.6 %reduce_sum.9 = f32[8]{0:T(128)} reduce(f32[8,128]{1,0:T(8,128)S(1)} %get-tuple-element.14, f32[]{:T(128)} %constant.0.clone.1), dimensions={1}, to_apply=%region_0.0 | reduce | flops 1016 | bytes 4132 | tf_op jit(solution)/shard_map/reduce_sum | solution.py:456
  48.0 0.8 %copy.16 = bf16[1,256,1024]{2,1,0:T(8,128)(2,1)} copy(bf16[1,256,1024]{2,1,0:T(8,128)(2,1)S(1)} %get-tuple-element.16) | data formatting | bytes 1048576
  48.7 0.8 %copy.17 = bf16[1,256,1024]{2,1,0:T(8,128)(2,1)} copy(bf16[1,256,1024]{2,1,0:T(8,128)(2,1)S(1)} %get-tuple-element.17) | data formatting | bytes 1048576
  49.5 0.8 %copy.18 = bf16[1,256,1024]{2,1,0:T(8,128)(2,1)} copy(bf16[1,256,1024]{2,1,0:T(8,128)(2,1)S(1)} %get-tuple-element.18) | data formatting | bytes 1048576

commit v7 on v5

--- a/solution.py
+++ b/solution.py
@@ -10,7 +10,7 @@
 WINDOW = 512
 HEAD = 128
 STRIP = 32
-AHEAD = 3
+AHEAD = 4
 LINE = 8
 MESH = pl.DeviceIdType.MESH
 

time: 50.9 us -> 50.9 us (level)
  no operation moved by 1% of the time
where the time goes in v7:
time: 50.9 us; the launch traced here: 50.7 us
  Pallas kernels  46.2 us (91%)
  local copies, waits for them, and re-layouts  3.17 us (6%)
  between operations  0.64 us (1%)
  other arithmetic  0.62 us (1%)
    pallas_call x1, Pallas kernels, shards(): pl.pallas_call(body, out_shape=(in_vmem,) * 4 + (pltpu.VMEM((heads, HEAD)...  46.2 us
    unnamed x4, local copies, waits for them, and re-layouts  3.17 us

profile of v7, /device:TPU:1, one launch (start us, length us, event | category | flops | bytes accessed | tf_op | source)
XLA Modules:
  0.0 50.7 jit_solution(15845794888893070535)
XLA Ops:
  0.6 46.2 %shard_map.101 = (bf16[1,256,1024]{2,1,0:T(8,128)(2,1)S(1)}, bf16[1,256,1024]{2,1,0:T(8,128)(2,1)S(1)}, bf16[1,256,1024]{2,1,0:T(8,128)(2,1)S(1)}, bf16[1,256,1024]{2,1,0:T(8,128)(2,1)S(1)}, f32[8,128]{1,0:T(8,128)S(1)}) custom-call(s32[1,17]{1,0:T(1,128)} %refs_0_.1, f32[8]{0:T(128)} %refs_1_.1, bf16[1,256,1024]{2,1,0:T(8,128)(2,1)} %refs_2_.1, ...), custom_call_target="tpu_custom_call" | custom-call | flops 3221225472 | bytes 2097152 | tf_op jit(solution)/shard_map/pallas_call | solution.py:411
  46.9 0.8 %copy.15 = bf16[1,256,1024]{2,1,0:T(8,128)(2,1)} copy(bf16[1,256,1024]{2,1,0:T(8,128)(2,1)S(1)} %get-tuple-element.15) | data formatting | bytes 1048576
  47.7 0.6 %reduce_sum.9 = f32[8]{0:T(128)} reduce(f32[8,128]{1,0:T(8,128)S(1)} %get-tuple-element.14, f32[]{:T(128)} %constant.0.clone.1), dimensions={1}, to_apply=%region_0.0 | reduce | flops 1016 | bytes 4132 | tf_op jit(solution)/shard_map/reduce_sum | solution.py:450
  48.3 0.8 %copy.16 = bf16[1,256,1024]{2,1,0:T(8,128)(2,1)} copy(bf16[1,256,1024]{2,1,0:T(8,128)(2,1)S(1)} %get-tuple-element.16) | data formatting | bytes 1048576
  49.1 0.8 %copy.17 = bf16[1,256,1024]{2,1,0:T(8,128)(2,1)} copy(bf16[1,256,1024]{2,1,0:T(8,128)(2,1)S(1)} %get-tuple-element.17) | data formatting | bytes 1048576
  49.9 0.8 %copy.18 = bf16[1,256,1024]{2,1,0:T(8,128)(2,1)} copy(bf16[1,256,1024]{2,1,0:T(8,128)(2,1)S(1)} %get-tuple-element.18) | data formatting | bytes 1048576
